TPU v7x, 32 devices: a whole 2x2x4 slice. The times are simulated.
32 devices in a mesh: rep: 4 (over y, x), shard: 8 (over z, core).
Axes of the slice: x: 2, y: 2, z: 4, core: 2. Of those that a mesh axis runs over, the one named last changes fastest.
Arguments:
- queries: bfloat16 [4, 1024, 2048], P('rep', 'shard'), may hold values from -6 to 6
- keys: bfloat16 [4, 1024, 256], P('rep', 'shard'), may hold values from -6 to 6
- values: bfloat16 [4, 1024, 256], P('rep', 'shard'), may hold values from -6 to 6
- segments: int32 [4, 1024], P('rep', 'shard'), may hold values from 0 to 15, never falling along the last dimension, each value on 1 to 512 neighbouring positions
- grad_output: bfloat16 [4, 1024, 1024], P('rep', 'shard'), may hold values from -0.375 to 0.375
Outputs:
- attention: bfloat16 [4, 1024, 2048], P('rep', 'shard')
- grad_weight: float32 [1024, 2048], P('shard')
Inputs may be any that keep to these rules, and one draw needn't show every extreme that they name: `segments`: document numbers never fall along a packed row; every document holds 1 to 512 positions and some document holds exactly 512.
All inputs are finite; a program needn't handle non-finite values.
Results may differ from a plain program's by a relative error of at most 0.015.
Values may be sent and summed in bfloat16 or wider, within the bound.
A program may use at most 64 MiB of HBM per device.

v0:
```python
import jax
import jax.numpy as jnp
from jax import lax
from jax.sharding import PartitionSpec as P

HEADS = 16
KVH = 2
HD = 128
SPAN = 4


def shifted(value, axis, steps):
    count = lax.axis_size(axis)
    first, last = (max(0, -steps), min(count, count - steps))
    return lax.ppermute(value, axis, [(source, source + steps) for source in range(first, last)])


def absorb(state_now, block_data, first_row, q_heads, q_seg, q_pos):
    running_max, weight_sum, accumulated = state_now
    key_part, value_part, seg_part = block_data
    row_count = key_part.shape[1]
    key_heads = key_part[0].reshape(row_count, KVH, HD)
    value_heads = value_part[0].reshape(row_count, KVH, HD).astype(jnp.float32)
    k_pos = first_row + jnp.arange(row_count, dtype=jnp.int32)
    allowed = (
        (q_seg[:, None] == seg_part[0][None, :])
        & (k_pos[None, :] <= q_pos[:, None])
        & (k_pos[None, :] >= 0)
    )
    scores = jnp.einsum(
        "qhgd,khd->hgqk", q_heads, key_heads, preferred_element_type=jnp.float32
    ) * HD ** (-0.5)
    scores = jnp.where(allowed, scores, -1e30)
    new_max = jnp.maximum(running_max, jnp.max(scores, axis=-1))
    weights = jnp.where(allowed, jnp.exp(scores - new_max[..., None]), 0.0)
    rescale = jnp.exp(running_max - new_max)
    weight_sum = weight_sum * rescale + jnp.sum(weights, axis=-1)
    product = jnp.einsum("hgqk,khd->hgqd", weights, value_heads, precision=lax.Precision.HIGHEST)
    accumulated = accumulated * rescale[..., None] + product
    return (new_max, weight_sum, accumulated)


def maybe_absorb(state_now, block_data, first_row, q_heads, q_seg, q_pos):
    return absorb(state_now, block_data, first_row, q_heads, q_seg, q_pos)


def local(queries, keys, values, segments, grad_output):
    tok_rows = queries.shape[1]
    shard_index = lax.axis_index("shard")
    group_size = HEADS // KVH
    q_heads = queries[0].reshape(tok_rows, KVH, group_size, HD)
    q_seg = segments[0]
    q_pos = shard_index * tok_rows + jnp.arange(tok_rows, dtype=jnp.int32)
    state_now = (
        jnp.full((KVH, group_size, tok_rows), -1e30, jnp.float32),
        jnp.zeros((KVH, group_size, tok_rows), jnp.float32),
        jnp.zeros((KVH, group_size, tok_rows, HD), jnp.float32),
    )
    own_block = (keys, values, segments)
    state_now = maybe_absorb(state_now, own_block, shard_index * tok_rows, q_heads, q_seg, q_pos)
    for distance in range(1, SPAN + 1):
        moved = shifted((keys, values, segments), "shard", distance)
        state_now = maybe_absorb(
            state_now, moved, (shard_index - distance) * tok_rows, q_heads, q_seg, q_pos
        )
    running_max, weight_sum, accumulated = state_now
    mixed = accumulated / weight_sum[..., None]
    attn_rows = (
        jnp.transpose(mixed, (2, 0, 1, 3)).reshape(tok_rows, HEADS * HD).astype(jnp.bfloat16)
    )
    grad_rows_local = grad_output[0]
    partial_value = lax.dot_general(
        grad_rows_local, attn_rows, (((0,), (0,)), ((), ())), preferred_element_type=jnp.float32
    )
    row_share = lax.psum_scatter(
        partial_value.astype(jnp.bfloat16), "shard", scatter_dimension=0, tiled=True
    ).astype(jnp.float32)
    grad_weight = lax.psum(row_share, "rep")
    return (attn_rows[None], grad_weight)


def solution(mesh):
    placed = (
        P("rep", "shard", None),
        P("rep", "shard", None),
        P("rep", "shard", None),
        P("rep", "shard"),
        P("rep", "shard", None),
    )
    return jax.shard_map(
        local,
        mesh=mesh,
        in_specs=placed,
        out_specs=(P("rep", "shard", None), P("shard", None)),
        check_vma=False,
    )
```

profile of v0, /device:TPU:0, one launch (start us, length us, event | category | flops | bytes accessed | tf_op | source)
XLA Modules:
  0.0 170.4 jit_solution(5971079050979282471)
XLA Ops:
  7.2 0.0 copy-start
  7.2 0.0 reduce-scatter.4.cloned.1.call-start
  7.2 5.1 %collective-permute-start.3 = (s32[1,128]{1,0:T(1,128)}, s32[1,128]{1,0:T(1,128)S(1)}, u32[]{:S(2)}, u32[]{:S(2)}) collective-permute-start(s32[1,128]{1,0:T(1,128)} %param.8), channel_id=1, source_target_pairs={{0,2},{1,3},{2,4},{3,5},{4,6},{5,7},{8,10},{9,11},{10,12},{11,13},... | collective-permute-start | bytes 1544 | tf_op jit(solution)/shard_map/ppermute | solution.py:15
  12.3 1.5 collective-permute-start
  13.8 5.0 %collective-permute-start.9 = (s32[1,128]{1,0:T(1,128)}, s32[1,128]{1,0:T(1,128)S(1)}, u32[]{:S(2)}, u32[]{:S(2)}) collective-permute-start(s32[1,128]{1,0:T(1,128)} %param.8), channel_id=1, source_target_pairs={{0,4},{1,5},{2,6},{3,7},{8,12},{9,13},{10,14},{11,15},{16,20},{17,... | collective-permute-start | bytes 1544 | tf_op jit(solution)/shard_map/ppermute | solution.py:15
  18.7 1.6 collective-permute-start.6
  20.3 1.6 copy.55
  21.9 2.3 %collective-permute-start.10 = (bf16[1,128,256]{1,2,0:T(8,128)(2,1)}, bf16[1,128,256]{1,2,0:T(8,128)(2,1)}, u32[]{:S(2)}, u32[]{:S(2)}) collective-permute-start(bf16[1,128,256]{1,2,0:T(8,128)(2,1)} %copy.55), channel_id=1, source_target_pairs={{0,4},{1,5},{2,6},{3,7},{8,12},{9,13},{10,14},{11,15},{16,20},{17,... | collective-permute-start | bytes 196616 | tf_op jit(solution)/shard_map/ppermute | solution.py:15
  24.3 0.9 reshape_squeeze.33
  25.1 1.0 copy.94
  26.1 1.2 copy.105
  27.2 0.0 collective-permute-done.3
  27.2 1.6 collective-permute-start.7
  28.8 1.3 collective-permute-start.4
  30.1 0.0 collective-permute-done.9
  30.1 2.6 %collective-permute-start.1 = (bf16[1,128,256]{1,2,0:T(8,128)(2,1)}, bf16[1,128,256]{1,2,0:T(8,128)(2,1)S(1)}, u32[]{:S(2)}, u32[]{:S(2)}) collective-permute-start(bf16[1,128,256]{1,2,0:T(8,128)(2,1)} %copy.55), channel_id=1, source_target_pairs={{0,1},{1,2},{2,3},{3,4},{4,5},{5,6},{6,7},{8,9},{9,10},{10,11},{11... | collective-permute-start | bytes 196616 | tf_op jit(solution)/shard_map/ppermute | solution.py:15
  32.8 2.8 %collective-permute-start.5 = (bf16[1,128,256]{2,1,0:T(8,128)(2,1)}, bf16[1,128,256]{2,1,0:T(8,128)(2,1)}, u32[]{:S(2)}, u32[]{:S(2)}) collective-permute-start(bf16[1,128,256]{2,1,0:T(8,128)(2,1)} %param.7), channel_id=1, source_target_pairs={{0,2},{1,3},{2,4},{3,5},{4,6},{5,7},{8,10},{9,11},{10,12},{11,13},... | collective-permute-start | bytes 196616 | tf_op jit(solution)/shard_map/ppermute | solution.py:15
  35.6 1.0 and_and_fusion.2
  36.7 0.3 fusion.69
  37.0 2.3 %collective-permute-start.2 = (bf16[1,128,256]{2,1,0:T(8,128)(2,1)}, bf16[1,128,256]{2,1,0:T(8,128)(2,1)}, u32[]{:S(2)}, u32[]{:S(2)}) collective-permute-start(bf16[1,128,256]{2,1,0:T(8,128)(2,1)} %param.7), channel_id=1, source_target_pairs={{0,1},{1,2},{2,3},{3,4},{4,5},{5,6},{6,7},{8,9},{9,10},{10,11},{11... | collective-permute-start | bytes 196616 | tf_op jit(solution)/shard_map/ppermute | solution.py:15
  39.3 0.4 fusion.68
  39.7 1.9 %collective-permute-start.11 = (bf16[1,128,256]{2,1,0:T(8,128)(2,1)}, bf16[1,128,256]{2,1,0:T(8,128)(2,1)}, u32[]{:S(2)}, u32[]{:S(2)}) collective-permute-start(bf16[1,128,256]{2,1,0:T(8,128)(2,1)} %param.7), channel_id=1, source_target_pairs={{0,4},{1,5},{2,6},{3,7},{8,12},{9,13},{10,14},{11,15},{16,20},{17,... | collective-permute-start | bytes 196616 | tf_op jit(solution)/shard_map/ppermute | solution.py:15
  41.6 0.4 fusion.67
  42.0 1.9 %collective-permute-start.8 = (bf16[1,128,256]{2,1,0:T(8,128)(2,1)}, bf16[1,128,256]{2,1,0:T(8,128)(2,1)}, u32[]{:S(2)}, u32[]{:S(2)}) collective-permute-start(bf16[1,128,256]{2,1,0:T(8,128)(2,1)} %param.7), channel_id=1, source_target_pairs={{0,3},{1,4},{2,5},{3,6},{4,7},{8,11},{9,12},{10,13},{11,14},{12,15... | collective-permute-start | bytes 196616 | tf_op jit(solution)/shard_map/ppermute | solution.py:15
  43.9 0.4 fusion.66
  44.3 1.2 fusion.65
  45.5 0.9 copy-done.1
  46.5 0.2 fusion.25
  46.7 0.4 fusion.23
  47.1 0.4 fusion.21
  47.5 0.6 bitcast_add_fusion
  48.1 1.8 %fusion.9 = f32[128,2,8,128]{0,3,2,1:T(8,128)} fusion(bf16[128,2,128,1]{0,2,3,1:T(8,128)(2,1)S(1)} %bitcast.229, f32[2,8,128,128]{2,3,1,0:T(8,128)S(1)} %get-tuple-element.33, f32[128,2,8]{0,2,1:T(8,128)S(1)} %get-tuple-element.16, f32[2,8,128]{2,1,0:T(8,128)S(1)} %get-tuple-element.18, f32[128,2,8]{0,2,1:T(8,128)S(1)} %get-tuple-element.17, ...), kind=kOutput, calls=%fused_computation.15 | convolution fusion | flops 403701760 | bytes 2203648 | tf_op jit(solution)/shard_map/hgqk,khd->hgqd/dot_general | solution.py:38
  49.9 0.9 copy.58
  50.9 3.0 %fusion.7 = f32[128,2,8,128]{0,3,2,1:T(8,128)} fusion(f32[128,2,8,128]{0,3,2,1:T(8,128)} %fusion.9, bf16[128,2,128,1]{0,2,3,1:T(8,128)(2,1)S(1)} %bitcast.231, f32[2,8,128,128]{2,3,1,0:T(8,128)S(1)} %get-tuple-element.31, f32[128,2,8]{0,2,1:T(8,128)} %get-tuple-element.11, f32[2,8,128]{2,1,0:T(8,128)} %copy-done.2, pred[128,128]{0,1:T(8,128)(4,1)S(1)} %get-tuple-element.23), kind=kOutput, calls=%fused_computation.12 | convolution fusion | flops 403701760 | bytes 3244032 | tf_op jit(solution)/shard_map/hgqk,khd->hgqd/dot_general | solution.py:38
  53.9 1.0 copy.63
  54.9 2.1 %fusion.5 = f32[128,2,8,128]{0,3,2,1:T(8,128)S(1)} fusion(f32[128,2,8,128]{0,3,2,1:T(8,128)} %fusion.7, bf16[128,2,128,1]{0,2,3,1:T(8,128)(2,1)S(1)} %bitcast.232, f32[2,8,128,128]{2,3,1,0:T(8,128)S(1)} %get-tuple-element.29, f32[128,2,8]{0,2,1:T(8,128)} %get-tuple-element.10, f32[2,8,128]{2,1,0:T(8,128)S(1)} %get-tuple-element.14, ...), kind=kOutput, calls=%fused_computation.9 | convolution fusion | flops 403701760 | bytes 3244032 | tf_op jit(solution)/shard_map/hgqk,khd->hgqd/dot_general | solution.py:38
  57.0 0.9 copy.68
  58.0 1.5 fusion.3
  59.5 0.9 copy.73
  60.5 2.1 %fusion.20 = bf16[128,2,8,128]{0,3,2,1:T(8,128)(2,1)S(1)} fusion(f32[128,2,8,128]{0,3,2,1:T(8,128)S(1)} %fusion.3, bf16[128,2,128,1]{0,2,3,1:T(8,128)(2,1)S(1)} %bitcast.237, f32[2,8,128,128]{2,3,1,0:T(8,128)} %copy-done.1, f32[128,2,8]{0,2,1:T(8,128)S(1)} %copy-done.5, f32[2,8,128]{2,1,0:T(8,128)S(1)} %copy-done.4, pred[128,128]{0,1:T(8,128)(4,1)S(1)} %get-tuple-element.21), kind=kOutput, calls=%fused_computation.31 | convolution fusion | flops 403963904 | bytes 2719744 | tf_op jit(solution)/shard_map/hgqk,khd->hgqd/dot_general | solution.py:38
  62.6 3.2 %convert_bitcast_fusion = bf16[1024,2048]{0,1:T(8,128)(2,1)} fusion(bf16[128,2048]{0,1:T(8,128)(2,1)S(1)} %bitcast.226, bf16[1,128,1024]{2,1,0:T(8,128)(2,1)S(1)} %copy-done), kind=kOutput, calls=%fused_computation | convolution fusion | flops 538968064 | bytes 4980736 | tf_op jit(solution)/shard_map/dot_general | solution.py:72
  65.8 6.5 %copy.103 = bf16[1024,2048]{1,0:T(8,128)(2,1)} copy(bf16[1024,2048]{0,1:T(8,128)(2,1)} %convert_bitcast_fusion) | data formatting | bytes 8388608
  72.3 0.0 reduce-scatter.4.cloned.1.call-update
  72.3 1.0 copy.75
  73.3 47.4 %reduce-scatter.4.cloned.1.call-done = bf16[128,2048]{1,0:T(8,128)(2,1)} async-done(((bf16[1024,2048]{1,0:T(8,128)(2,1)}), bf16[128,2048]{1,0:T(8,128)(2,1)}) %reduce-scatter.4.cloned.1.call-update) | async-done | bytes 524304
  120.7 1.3 copy.104
  122.0 40.2 %all-reduce.1 = f32[128,2048]{0,1:T(8,128)S(1)} all-reduce(bf16[128,2048]{0,1:T(8,128)(2,1)S(1)} %copy.104), channel_id=1, replica_groups=mesh['rep'=4,'shard'=8] {'rep'}, use_global_device_ids=true, to_apply=%region_11.12 | all-reduce | flops 262144 | bytes 1572864 | tf_op jit(solution)/shard_map/psum | solution.py:78
  162.3 1.3 copy.76
  (31 shorter events, 0.1 us)
Async XLA Ops:
  7.2 55.4 %copy-start = (bf16[1,128,1024]{2,1,0:T(8,128)(2,1)S(1)}, bf16[1,128,1024]{2,1,0:T(8,128)(2,1)}, u32[]{:S(2)}) copy-start(bf16[1,128,1024]{2,1,0:T(8,128)(2,1)} %param.9) | copy-start | bytes 786436
  7.2 113.5 %reduce-scatter.4.cloned.1.call-start = ((), (), s32[]{:S(2)}) async-start(), calls=%async_computation.1 | async-start | bytes 4718592
  7.2 20.0 %collective-permute-start.3 = (s32[1,128]{1,0:T(1,128)}, s32[1,128]{1,0:T(1,128)S(1)}, u32[]{:S(2)}, u32[]{:S(2)}) collective-permute-start(s32[1,128]{1,0:T(1,128)} %param.8), channel_id=1, source_target_pairs={{0,2},{1,3},{2,4},{3,5},{4,6},{5,7},{8,10},{9,11},{10,12},{11,13},... | collective-permute-start | bytes 1544 | tf_op jit(solution)/shard_map/ppermute | solution.py:15
  12.3 16.5 %collective-permute-start = (s32[1,128]{1,0:T(1,128)}, s32[1,128]{1,0:T(1,128)S(1)}, u32[]{:S(2)}, u32[]{:S(2)}) collective-permute-start(s32[1,128]{1,0:T(1,128)} %param.8), channel_id=1, source_target_pairs={{0,1},{1,2},{2,3},{3,4},{4,5},{5,6},{6,7},{8,9},{9,10},{10,11},{11... | collective-permute-start | bytes 1544 | tf_op jit(solution)/shard_map/ppermute | solution.py:15
  13.8 16.4 %collective-permute-start.9 = (s32[1,128]{1,0:T(1,128)}, s32[1,128]{1,0:T(1,128)S(1)}, u32[]{:S(2)}, u32[]{:S(2)}) collective-permute-start(s32[1,128]{1,0:T(1,128)} %param.8), channel_id=1, source_target_pairs={{0,4},{1,5},{2,6},{3,7},{8,12},{9,13},{10,14},{11,15},{16,20},{17,... | collective-permute-start | bytes 1544 | tf_op jit(solution)/shard_map/ppermute | solution.py:15
  18.7 14.1 %collective-permute-start.6 = (s32[1,128]{1,0:T(1,128)}, s32[1,128]{1,0:T(1,128)S(1)}, u32[]{:S(2)}, u32[]{:S(2)}) collective-permute-start(s32[1,128]{1,0:T(1,128)} %param.8), channel_id=1, source_target_pairs={{0,3},{1,4},{2,5},{3,6},{4,7},{8,11},{9,12},{10,13},{11,14},{12,15... | collective-permute-start | bytes 1544 | tf_op jit(solution)/shard_map/ppermute | solution.py:15
  21.9 22.4 %collective-permute-start.10 = (bf16[1,128,256]{1,2,0:T(8,128)(2,1)}, bf16[1,128,256]{1,2,0:T(8,128)(2,1)}, u32[]{:S(2)}, u32[]{:S(2)}) collective-permute-start(bf16[1,128,256]{1,2,0:T(8,128)(2,1)} %copy.55), channel_id=1, source_target_pairs={{0,4},{1,5},{2,6},{3,7},{8,12},{9,13},{10,14},{11,15},{16,20},{17,... | collective-permute-start | bytes 196616 | tf_op jit(solution)/shard_map/ppermute | solution.py:15
  27.2 14.7 %collective-permute-start.7 = (bf16[1,128,256]{1,2,0:T(8,128)(2,1)}, bf16[1,128,256]{1,2,0:T(8,128)(2,1)S(1)}, u32[]{:S(2)}, u32[]{:S(2)}) collective-permute-start(bf16[1,128,256]{1,2,0:T(8,128)(2,1)} %copy.55), channel_id=1, source_target_pairs={{0,3},{1,4},{2,5},{3,6},{4,7},{8,11},{9,12},{10,13},{11,14},{12,15... | collective-permute-start | bytes 196616 | tf_op jit(solution)/shard_map/ppermute | solution.py:15
  28.8 10.8 %collective-permute-start.4 = (bf16[1,128,256]{1,2,0:T(8,128)(2,1)}, bf16[1,128,256]{1,2,0:T(8,128)(2,1)S(1)}, u32[]{:S(2)}, u32[]{:S(2)}) collective-permute-start(bf16[1,128,256]{1,2,0:T(8,128)(2,1)} %copy.55), channel_id=1, source_target_pairs={{0,2},{1,3},{2,4},{3,5},{4,6},{5,7},{8,10},{9,11},{10,12},{11,13},... | collective-permute-start | bytes 196616 | tf_op jit(solution)/shard_map/ppermute | solution.py:15
  30.1 6.9 %collective-permute-start.1 = (bf16[1,128,256]{1,2,0:T(8,128)(2,1)}, bf16[1,128,256]{1,2,0:T(8,128)(2,1)S(1)}, u32[]{:S(2)}, u32[]{:S(2)}) collective-permute-start(bf16[1,128,256]{1,2,0:T(8,128)(2,1)} %copy.55), channel_id=1, source_target_pairs={{0,1},{1,2},{2,3},{3,4},{4,5},{5,6},{6,7},{8,9},{9,10},{10,11},{11... | collective-permute-start | bytes 196616 | tf_op jit(solution)/shard_map/ppermute | solution.py:15
  32.8 21.1 %collective-permute-start.5 = (bf16[1,128,256]{2,1,0:T(8,128)(2,1)}, bf16[1,128,256]{2,1,0:T(8,128)(2,1)}, u32[]{:S(2)}, u32[]{:S(2)}) collective-permute-start(bf16[1,128,256]{2,1,0:T(8,128)(2,1)} %param.7), channel_id=1, source_target_pairs={{0,2},{1,3},{2,4},{3,5},{4,6},{5,7},{8,10},{9,11},{10,12},{11,13},... | collective-permute-start | bytes 196616 | tf_op jit(solution)/shard_map/ppermute | solution.py:15
  37.0 12.9 %collective-permute-start.2 = (bf16[1,128,256]{2,1,0:T(8,128)(2,1)}, bf16[1,128,256]{2,1,0:T(8,128)(2,1)}, u32[]{:S(2)}, u32[]{:S(2)}) collective-permute-start(bf16[1,128,256]{2,1,0:T(8,128)(2,1)} %param.7), channel_id=1, source_target_pairs={{0,1},{1,2},{2,3},{3,4},{4,5},{5,6},{6,7},{8,9},{9,10},{10,11},{11... | collective-permute-start | bytes 196616 | tf_op jit(solution)/shard_map/ppermute | solution.py:15
  39.7 19.8 %collective-permute-start.11 = (bf16[1,128,256]{2,1,0:T(8,128)(2,1)}, bf16[1,128,256]{2,1,0:T(8,128)(2,1)}, u32[]{:S(2)}, u32[]{:S(2)}) collective-permute-start(bf16[1,128,256]{2,1,0:T(8,128)(2,1)} %param.7), channel_id=1, source_target_pairs={{0,4},{1,5},{2,6},{3,7},{8,12},{9,13},{10,14},{11,15},{16,20},{17,... | collective-permute-start | bytes 196616 | tf_op jit(solution)/shard_map/ppermute | solution.py:15
  42.0 15.0 %collective-permute-start.8 = (bf16[1,128,256]{2,1,0:T(8,128)(2,1)}, bf16[1,128,256]{2,1,0:T(8,128)(2,1)}, u32[]{:S(2)}, u32[]{:S(2)}) collective-permute-start(bf16[1,128,256]{2,1,0:T(8,128)(2,1)} %param.7), channel_id=1, source_target_pairs={{0,3},{1,4},{2,5},{3,6},{4,7},{8,11},{9,12},{10,13},{11,14},{12,15... | collective-permute-start | bytes 196616 | tf_op jit(solution)/shard_map/ppermute | solution.py:15
  45.5 1.0 copy-start.1
  45.5 1.2 copy-start.3
  45.5 4.4 %copy-start.2 = (f32[2,8,128]{2,1,0:T(8,128)}, f32[2,8,128]{2,1,0:T(8,128)S(1)}, u32[]{:S(2)}) copy-start(f32[2,8,128]{2,1,0:T(8,128)S(1)} %get-tuple-element.15) | copy-start | bytes 24580
  53.9 6.5 %copy-start.4 = (f32[2,8,128]{2,1,0:T(8,128)S(1)}, f32[2,8,128]{2,1,0:T(8,128)}, u32[]{:S(2)}) copy-start(f32[2,8,128]{2,1,0:T(8,128)} %copy-done.3) | copy-start | bytes 24580
  53.9 6.5 %copy-start.5 = (f32[128,2,8]{0,2,1:T(8,128)S(1)}, f32[128,2,8]{0,2,1:T(8,128)}, u32[]{:S(2)}) copy-start(f32[128,2,8]{0,2,1:T(8,128)} %get-tuple-element.8) | copy-start | bytes 24580
Sparse Core Ops, SparseCore 0:
  72.4 48.2 reduce-scatter.3
where the time goes:
time: 172 us; the launch traced here: 170 us
  waiting for transfers between devices  47.4 us (28%)
  blocking collectives  40.2 us (23%)
  starting transfers between devices  29.8 us (17%)
  local copies, waits for them, and re-layouts  19.4 us (11%)
  matrix products  16.3 us (9%)
  between operations  14.4 us (8%)
  other arithmetic  2.77 us (2%)
    unnamed x2, waiting for transfers between devices  47.4 us
    psum x1, blocking collectives, local(): grad_weight = lax.psum(row_share, 'rep')  40.2 us
    ppermute x12, starting transfers between devices, shifted(): lax.ppermute(value, axis, [(source, source + steps) for source in range(f...  29.7 us
    unnamed x18, local copies, waits for them, and re-layouts  13.8 us
    dot_general x5, matrix products, absorb(): jnp.einsum('hgqk,khd->hgqd', weights, value_heads, precision=lax.Precisio...  10.5 us
    ppermute x4, local copies, waits for them, and re-layouts, shifted(): lax.ppermute(value, axis, [(source, source + steps) for source in range(f...  3.82 us
  transfers between devices with their start and end apart: 13, of which 1 were waited for; matrix products, arithmetic and copies ran while one was open for 13% of the time, Pallas kernels for 0%

commit v1 on v0

v1 whole, which is shorter than its diff:
```python
import functools

import jax
import jax.numpy as jnp
from jax import lax
from jax.experimental import pallas as pl
from jax.experimental.pallas import tpu as pltpu
from jax.sharding import PartitionSpec as P

HEADS = 16
KVH = 2
HD = 128
MOST = 512
MESH = pl.DeviceIdType.MESH
F32 = jnp.float32
BF16 = jnp.bfloat16
SCALE = HD ** (-0.5) * 1.4426950408889634


def kernel(
    n_rep, n_shard,
    q_ref, k_ref, v_ref, seg_ref, g_ref,
    attn_ref, gw_ref,
    kv, kext, vext, bias, gt_out, gt, a_all, p_out, z_in, o_all,
    zk_send, zk_recv, sb_send, sb_recv, g_send, g_recv, a_send, a_recv,
    p_send, p_recv, o_send, o_recv,
):
    rows = q_ref.shape[0]
    span = MOST // rows
    reach = span // 2
    n_chip = n_shard // 2
    out_rows = g_ref.shape[1] // n_shard
    heads_each = HEADS // n_rep
    width = heads_each * HD
    rep = lax.axis_index("rep")
    me = lax.axis_index("shard")
    core = lax.rem(me, 2)
    chip = me // 2
    sib = me + 1 - 2 * core
    other = 1 - core
    slot = rep * 2 + core
    sib_slot = rep * 2 + other

    def remote(src, dst, send_sem, recv_sem, to_rep, to_shard):
        return pltpu.make_async_remote_copy(
            src_ref=src, dst_ref=dst, send_sem=send_sem, recv_sem=recv_sem,
            device_id=(to_rep, to_shard), device_id_type=MESH,
        )

    def rep_at(step):
        return lax.rem(rep + step, n_rep)

    def chip_at(step):
        return lax.rem(chip + step, n_chip)

    barrier = pltpu.get_barrier_semaphore()
    pl.semaphore_signal(barrier, inc=1, device_id=(rep, sib), device_id_type=MESH)
    for step in range(1, n_chip):
        pl.semaphore_signal(
            barrier, inc=1, device_id=(rep, chip_at(step) * 2 + core), device_id_type=MESH
        )
    for step in range(1, n_rep):
        for side in range(2):
            pl.semaphore_signal(
                barrier, inc=1, device_id=(rep_at(step), chip * 2 + side), device_id_type=MESH
            )
    seg_row = seg_ref[...].astype(F32)
    kv[span, 0:rows, 0:KVH * HD] = k_ref[...]
    kv[span, 0:rows, KVH * HD:2 * KVH * HD] = v_ref[...]
    kv[span, rows:rows + 16, :] = jnp.zeros((16, 2 * KVH * HD), BF16)
    kv[span, rows:rows + 16, 0:rows] = jnp.broadcast_to(seg_row, (16, rows)).astype(BF16)
    for place in range(span):
        @pl.when(me - span + place < 0)
        def _(place=place):
            kv[place] = jnp.zeros(kv.shape[1:], BF16)
    pl.semaphore_wait(barrier, 1 + (n_chip - 1) + 2 * (n_rep - 1))

    def along(d):
        return remote(
            kv.at[span], kv.at[span - 2 * d], zk_send.at[d - 1], zk_recv.at[d - 1],
            rep, me + 2 * d,
        )

    for d in range(1, reach + 1):
        @pl.when(chip + d < n_chip)
        def _(d=d):
            along(d).start()

    def across(d):
        place = span + 1 - 2 * d
        return remote(
            kv.at[place + 1 - 2 * core], kv.at[place], sb_send.at[d - 1], sb_recv.at[d - 1],
            rep, sib,
        )

    def across_exists(d):
        return sib - 2 * d + 1 >= 0

    @pl.when(core == 0)
    def _():
        across(1).start()

    for b in range(n_shard):
        if (b * out_rows) % 128 == 0:
            take = max(out_rows, 128)
            piece = g_ref[:, b * out_rows:b * out_rows + take].astype(F32).T.astype(BF16)
        lead = (b * out_rows) % 128 if out_rows < 128 else 0
        gt_out[b % 2, (b // 2) * out_rows:(b // 2 + 1) * out_rows, :] = piece[lead:lead + out_rows]

    def g_copy(step, side):
        return remote(
            gt_out.at[side], gt.at[:, pl.ds(pl.multiple_of(slot * rows, 128), rows)],
            g_send.at[2 * step + side], g_recv.at[slot], rep_at(step), chip * 2 + side,
        )

    for step in range(1, n_rep):
        for side in range(2):
            g_copy(step, side).start()
    g_sib = remote(
        gt_out.at[other], gt.at[:, pl.ds(pl.multiple_of(slot * rows, 128), rows)],
        g_send.at[0], g_recv.at[slot], rep, sib,
    )
    g_sib.start()
    gt[:, pl.ds(pl.multiple_of(slot * rows, 128), rows)] = gt_out[core]

    for d in range(1, reach + 1):
        @pl.when(chip >= d)
        def _(d=d):
            along(d).wait_recv()
        if d <= reach:
            @pl.when((core == 1) & across_exists(d))
            def _(d=d):
                across(d).start()
        if d + 1 <= reach:
            @pl.when((core == 0) & across_exists(d + 1))
            def _(d=d):
                across(d + 1).start()
    for d in range(1, reach + 1):
        @pl.when(me - 2 * d + 1 >= 0)
        def _(d=d):
            across(d).wait_recv()

    q_seg = jnp.broadcast_to(seg_row, (rows, rows)).T
    for place in range(span + 1):
        k_seg = kv[place, rows:rows + 16, 0:rows].astype(F32)[0:1]
        allowed = q_seg == k_seg
        if place == span:
            q_at = lax.broadcasted_iota(jnp.int32, (rows, rows), 0)
            k_at = lax.broadcasted_iota(jnp.int32, (rows, rows), 1)
            allowed = allowed & (k_at <= q_at)
        else:
            block = lax.broadcasted_iota(jnp.int32, (rows, rows), 0) * 0 + (me - span + place)
            allowed = allowed & (block >= 0)
        bias[:, place * rows:(place + 1) * rows] = jnp.where(allowed, 0.0, -1e30)
        for head in range(KVH):
            lo = head * HD
            span_rows = slice(place * rows, (place + 1) * rows)
            kext[head, span_rows, :] = kv[place, 0:rows, lo:lo + HD]
            vext[head, span_rows, 0:HD] = kv[place, 0:rows, KVH * HD + lo:KVH * HD + lo + HD]
            vext[head, span_rows, HD:2 * HD] = jnp.ones((rows, HD), BF16)

    def columns(step):
        return pl.ds(pl.multiple_of(rep_at(step) * width, 128), width)

    def a_copy(step, side):
        return remote(
            attn_ref.at[:, columns(step)], a_all.at[pl.ds(slot * rows, rows), :],
            a_send.at[2 * step + side], a_recv.at[slot], rep_at(step), chip * 2 + side,
        )

    a_sib = remote(
        attn_ref.at[:, columns(0)], a_all.at[pl.ds(slot * rows, rows), :],
        a_send.at[0], a_recv.at[slot], rep, sib,
    )
    for step in list(range(1, n_rep)) + [0]:
        for j in range(heads_each):
            head = rep_at(step) * heads_each + j
            group = head // (HEADS // KVH)
            lanes = pl.ds(pl.multiple_of(head * HD, 128), HD)
            s = lax.dot_general(
                q_ref[:, lanes], kext[group], (((1,), (1,)), ((), ())),
                preferred_element_type=F32,
            ) + bias[...]
            top = jnp.max(s, axis=-1, keepdims=True)
            p = jnp.exp2((s - top) * SCALE).astype(BF16)
            o = jnp.dot(p, vext[group], preferred_element_type=F32)
            mixed = (o[:, 0:HD] / o[:, HD:2 * HD]).astype(BF16)
            attn_ref[:, lanes] = mixed
            if step == 0:
                a_all[pl.ds(slot * rows, rows), j * HD:(j + 1) * HD] = mixed
        if step == 0:
            a_sib.start()
        else:
            for side in range(2):
                a_copy(step, side).start()

    def arrived(index):
        remote(
            gt_out.at[0], gt.at[:, pl.ds(pl.multiple_of(index * rows, 128), rows)],
            g_send.at[0], g_recv.at[index], rep, sib,
        ).wait_recv()
        remote(
            attn_ref.at[:, columns(0)], a_all.at[pl.ds(index * rows, rows), :],
            a_send.at[0], a_recv.at[index], rep, sib,
        ).wait_recv()

    arrived(sib_slot)
    for step in range(1, n_rep):
        for side in range(2):
            arrived(rep_at(n_rep - step) * 2 + side)

    def term(target):
        block = gt[pl.ds(pl.multiple_of(target * out_rows, 16), out_rows), :]
        return jnp.dot(block, a_all[...], preferred_element_type=F32)

    def p_copy(step):
        return remote(
            p_out.at[chip_at(step)], z_in.at[chip], p_send.at[step], p_recv.at[chip],
            rep, chip_at(step) * 2 + core,
        )

    for step in range(1, n_chip):
        p_out[chip_at(step)] = term(chip_at(step)).astype(BF16)
        p_copy(step).start()
    total = term(chip)
    for step in range(1, n_chip):
        source = chip_at(n_chip - step)
        remote(
            p_out.at[0], z_in.at[source], p_send.at[0], p_recv.at[source], rep, sib
        ).wait_recv()
        total = total + z_in[source].astype(F32)

    o_all[rep] = total.astype(BF16)

    def o_copy(step):
        return remote(
            o_all.at[rep], o_all.at[rep], o_send.at[step], o_recv.at[rep], rep_at(step), me
        )

    for step in range(1, n_rep):
        o_copy(step).start()
    gw_ref[:, columns(0)] = o_all[rep].astype(F32)
    for step in range(1, n_rep):
        source = rep_at(n_rep - step)
        remote(
            o_all.at[source], o_all.at[source], o_send.at[0], o_recv.at[source], rep, sib
        ).wait_recv()
        gw_ref[:, columns(n_rep - step)] = o_all[source].astype(F32)

    for d in range(1, reach + 1):
        @pl.when(chip + d < n_chip)
        def _(d=d):
            along(d).wait_send()

        @pl.when(across_exists(d))
        def _(d=d):
            across(d).wait_send()
    g_sib.wait_send()
    a_sib.wait_send()
    for step in range(1, n_rep):
        for side in range(2):
            g_copy(step, side).wait_send()
            a_copy(step, side).wait_send()
        o_copy(step).wait_send()
    for step in range(1, n_chip):
        p_copy(step).wait_send()


def local(queries, keys, values, segments, grad_output):
    n_rep, n_shard = lax.axis_size("rep"), lax.axis_size("shard")
    rows = queries.shape[1]
    span = MOST // rows
    reach = span // 2
    n_chip = n_shard // 2
    features = grad_output.shape[2]
    out_rows = features // n_shard
    width = HEADS * HD // n_rep
    vmem = pl.BlockSpec(memory_space=pltpu.VMEM)
    dma = pltpu.SemaphoreType.DMA
    attn, grad_weight = pl.pallas_call(
        functools.partial(kernel, n_rep, n_shard),
        out_shape=(
            jax.ShapeDtypeStruct((rows, HEADS * HD), BF16),
            jax.ShapeDtypeStruct((out_rows, HEADS * HD), F32),
        ),
        in_specs=[vmem] * 5,
        out_specs=(vmem, vmem),
        scratch_shapes=[
            pltpu.VMEM((span + 1, rows + 16, 2 * KVH * HD), BF16),
            pltpu.VMEM((KVH, (span + 1) * rows, HD), BF16),
            pltpu.VMEM((KVH, (span + 1) * rows, 2 * HD), BF16),
            pltpu.VMEM((rows, (span + 1) * rows), F32),
            pltpu.VMEM((2, features // 2, rows), BF16),
            pltpu.VMEM((features // 2, 2 * n_rep * rows), BF16),
            pltpu.VMEM((2 * n_rep * rows, width), BF16),
            pltpu.VMEM((n_chip, out_rows, width), BF16),
            pltpu.VMEM((n_chip, out_rows, width), BF16),
            pltpu.VMEM((n_rep, out_rows, width), BF16),
            dma((reach,)), dma((reach,)), dma((reach,)), dma((reach,)),
            dma((2 * n_rep,)), dma((2 * n_rep,)), dma((2 * n_rep,)), dma((2 * n_rep,)),
            dma((n_chip,)), dma((n_chip,)), dma((n_rep,)), dma((n_rep,)),
        ],
        compiler_params=pltpu.CompilerParams(
            collective_id=0, has_side_effects=True, vmem_limit_bytes=40 * 1024 * 1024
        ),
    )(queries[0], keys[0], values[0], segments, grad_output[0])
    return attn[None], grad_weight


def solution(mesh):
    placed = (
        P("rep", "shard", None),
        P("rep", "shard", None),
        P("rep", "shard", None),
        P("rep", "shard"),
        P("rep", "shard", None),
    )
    return jax.shard_map(
        local,
        mesh=mesh,
        in_specs=placed,
        out_specs=(P("rep", "shard", None), P("shard", None)),
        check_vma=False,
    )
```

time: 172 us -> 54.5 us (0.32)
  the two profiles are of different devices: /device:TPU:0 before, /device:TPU:27 now
where the time goes in v1:
time: 54.5 us; the launch traced here: 54.2 us
  Pallas kernels  47.5 us (87%)
  local copies, waits for them, and re-layouts  6.08 us (11%)
  between operations  0.65 us (1%)
    pallas_call x1, Pallas kernels, local(): pl.pallas_call(functools.partial(kernel, n_rep, n_shard), out_shape=(jax....  47.5 us
    unnamed x12, local copies, waits for them, and re-layouts  6.08 us

profile of v1, /device:TPU:27, one launch (start us, length us, event | category | flops | bytes accessed | tf_op | source)
XLA Modules:
  0.0 54.2 jit_solution(6247700316621584868)
XLA Ops:
  0.6 0.0 copy-start.4
  0.6 0.6 %copy-done.4 = s32[1,128]{1,0:T(1,128)S(1)} copy-done((s32[1,128]{1,0:T(1,128)S(1)}, s32[1,128]{1,0:T(1,128)}, u32[]{:S(2)}) %copy-start.4) | copy-done | bytes 536
  1.3 0.0 copy-start
  1.3 1.0 %copy-done = bf16[1,128,2048]{2,1,0:T(8,128)(2,1)S(1)} copy-done((bf16[1,128,2048]{2,1,0:T(8,128)(2,1)S(1)}, bf16[1,128,2048]{2,1,0:T(8,128)(2,1)}, u32[]{:S(2)}) %copy-start) | copy-done | bytes 524312
  2.3 0.0 copy-start.1
  2.3 0.9 %copy-done.1 = bf16[1,128,1024]{2,1,0:T(8,128)(2,1)S(1)} copy-done((bf16[1,128,1024]{2,1,0:T(8,128)(2,1)S(1)}, bf16[1,128,1024]{2,1,0:T(8,128)(2,1)}, u32[]{:S(2)}) %copy-start.1) | copy-done | bytes 262168
  3.3 0.0 copy-start.2
  3.3 0.8 %copy-done.2 = bf16[1,128,256]{2,1,0:T(8,128)(2,1)S(1)} copy-done((bf16[1,128,256]{2,1,0:T(8,128)(2,1)S(1)}, bf16[1,128,256]{2,1,0:T(8,128)(2,1)}, u32[]{:S(2)}) %copy-start.2) | copy-done | bytes 65560
  4.1 0.0 copy-start.3
  4.1 0.8 %copy-done.3 = bf16[1,128,256]{2,1,0:T(8,128)(2,1)S(1)} copy-done((bf16[1,128,256]{2,1,0:T(8,128)(2,1)S(1)}, bf16[1,128,256]{2,1,0:T(8,128)(2,1)}, u32[]{:S(2)}) %copy-start.3) | copy-done | bytes 65560
  5.0 47.5 %shard_map.68 = (bf16[128,2048]{1,0:T(8,128)(2,1)S(1)}, f32[128,2048]{1,0:T(8,128)S(1)}) custom-call(bf16[128,2048]{1,0:T(8,128)(2,1)S(1)} %bitcast.5, bf16[128,256]{1,0:T(8,128)(2,1)S(1)} %bitcast.8, bf16[128,256]{1,0:T(8,128)(2,1)S(1)} %bitcast.9, s32[1,128]{1,0:T(1,128)S(1)} %copy-done.4, bf16[128,1024]{1,0:T(8,128)(2,1)S(1)} %bitcast.7), custom_call_target="tpu_custom_call" | custom-call | tf_op jit(solution)/shard_map/pallas_call | solution.py:280
  52.5 0.8 %copy.9 = bf16[1,128,2048]{2,1,0:T(8,128)(2,1)} copy(bf16[1,128,2048]{2,1,0:T(8,128)(2,1)S(1)} %bitcast.6) | data formatting | bytes 1048576
  53.3 1.0 %copy.10 = f32[128,2048]{1,0:T(8,128)} copy(f32[128,2048]{1,0:T(8,128)S(1)} %get-tuple-element.9) | data formatting | bytes 2097152
Async XLA Ops:
  0.6 0.7 %copy-start.4 = (s32[1,128]{1,0:T(1,128)S(1)}, s32[1,128]{1,0:T(1,128)}, u32[]{:S(2)}) copy-start(s32[1,128]{1,0:T(1,128)} %seg_ref.1) | copy-start | bytes 1540
  1.3 1.0 %copy-start = (bf16[1,128,2048]{2,1,0:T(8,128)(2,1)S(1)}, bf16[1,128,2048]{2,1,0:T(8,128)(2,1)}, u32[]{:S(2)}) copy-start(bf16[1,128,2048]{2,1,0:T(8,128)(2,1)} %param.5) | copy-start | bytes 1572868
  2.3 0.9 %copy-start.1 = (bf16[1,128,1024]{2,1,0:T(8,128)(2,1)S(1)}, bf16[1,128,1024]{2,1,0:T(8,128)(2,1)}, u32[]{:S(2)}) copy-start(bf16[1,128,1024]{2,1,0:T(8,128)(2,1)} %param.9) | copy-start | bytes 786436
  3.3 0.8 %copy-start.2 = (bf16[1,128,256]{2,1,0:T(8,128)(2,1)S(1)}, bf16[1,128,256]{2,1,0:T(8,128)(2,1)}, u32[]{:S(2)}) copy-start(bf16[1,128,256]{2,1,0:T(8,128)(2,1)} %param.6) | copy-start | bytes 196612
  4.1 0.8 %copy-start.3 = (bf16[1,128,256]{2,1,0:T(8,128)(2,1)S(1)}, bf16[1,128,256]{2,1,0:T(8,128)(2,1)}, u32[]{:S(2)}) copy-start(bf16[1,128,256]{2,1,0:T(8,128)(2,1)} %param.7) | copy-start | bytes 196612

commit v2 on v1

--- a/solution.py
+++ b/solution.py
@@ -12,20 +12,22 @@
 HD = 128
 MOST = 512
 MESH = pl.DeviceIdType.MESH
+EARLY = 4
 F32 = jnp.float32
 BF16 = jnp.bfloat16
 SCALE = HD ** (-0.5) * 1.4426950408889634
 
 
-def kernel(
+def kernel_narrow(
     n_rep, n_shard,
-    q_ref, k_ref, v_ref, seg_ref, g_ref,
+    q_hbm, k_hbm, v_hbm, seg_hbm, g_hbm,
     attn_ref, gw_ref,
-    kv, kext, vext, bias, gt_out, gt, a_all, p_out, z_in, o_all,
+    q_ref, seg_ref, g_ref, in_sem, kv, kext, vext, bias, gt_out, gt, a_all, p_out, z_in, o_all,
     zk_send, zk_recv, sb_send, sb_recv, g_send, g_recv, a_send, a_recv,
     p_send, p_recv, o_send, o_recv,
 ):
     rows = q_ref.shape[0]
+    half = KVH * HD
     span = MOST // rows
     reach = span // 2
     n_chip = n_shard // 2
@@ -53,6 +55,19 @@
     def chip_at(step):
         return lax.rem(chip + step, n_chip)
 
+    loads = [
+        pltpu.make_async_copy(src, dst, in_sem.at[i])
+        for i, (src, dst) in enumerate([
+            (k_hbm, kv.at[span, 0:rows, 0:half]),
+            (v_hbm, kv.at[span, 0:rows, half:2 * half]),
+            (seg_hbm, seg_ref),
+            (g_hbm, g_ref),
+            (q_hbm, q_ref),
+        ])
+    ]
+    for load in loads:
+        load.start()
+
     barrier = pltpu.get_barrier_semaphore()
     pl.semaphore_signal(barrier, inc=1, device_id=(rep, sib), device_id_type=MESH)
     for step in range(1, n_chip):
@@ -64,15 +79,15 @@
             pl.semaphore_signal(
                 barrier, inc=1, device_id=(rep_at(step), chip * 2 + side), device_id_type=MESH
             )
-    seg_row = seg_ref[...].astype(F32)
-    kv[span, 0:rows, 0:KVH * HD] = k_ref[...]
-    kv[span, 0:rows, KVH * HD:2 * KVH * HD] = v_ref[...]
-    kv[span, rows:rows + 16, :] = jnp.zeros((16, 2 * KVH * HD), BF16)
-    kv[span, rows:rows + 16, 0:rows] = jnp.broadcast_to(seg_row, (16, rows)).astype(BF16)
     for place in range(span):
         @pl.when(me - span + place < 0)
         def _(place=place):
             kv[place] = jnp.zeros(kv.shape[1:], BF16)
+    kv[span, rows:rows + 16, :] = jnp.zeros((16, 2 * half), BF16)
+    for load in loads[:3]:
+        load.wait()
+    seg_row = seg_ref[...].astype(F32)
+    kv[span, rows:rows + 16, 0:rows] = jnp.broadcast_to(seg_row, (16, rows)).astype(BF16)
     pl.semaphore_wait(barrier, 1 + (n_chip - 1) + 2 * (n_rep - 1))
 
     def along(d):
@@ -99,6 +114,8 @@
     @pl.when(core == 0)
     def _():
         across(1).start()
+
+    loads[3].wait()
 
     for b in range(n_shard):
         if (b * out_rows) % 128 == 0:
@@ -158,6 +175,8 @@
             kext[head, span_rows, :] = kv[place, 0:rows, lo:lo + HD]
             vext[head, span_rows, 0:HD] = kv[place, 0:rows, KVH * HD + lo:KVH * HD + lo + HD]
             vext[head, span_rows, HD:2 * HD] = jnp.ones((rows, HD), BF16)
+
+    loads[4].wait()
 
     def columns(step):
         return pl.ds(pl.multiple_of(rep_at(step) * width, 128), width)
@@ -266,7 +285,308 @@
         p_copy(step).wait_send()
 
 
-def local(queries, keys, values, segments, grad_output):
+def kernel(
+    n_rep, n_shard,
+    q_hbm, k_hbm, v_hbm, seg_hbm, g_hbm,
+    attn_hbm, gw_ref,
+    q_ref, seg_ref, g_ref, in_sem, kv, kext, vext, bias, gt_out, gt, attn_vm, a_all, p_out, z_in, o_all,
+    zk_send, zk_recv, sb_send, sb_recv, g_send, g_recv, a_send, a_recv,
+    p_send, p_recv, o_send, o_recv, f_send, out_sem,
+):
+    rows = q_ref.shape[0]
+    half = KVH * HD
+    span = MOST // rows
+    reach = span // 2
+    n_chip = n_shard // 2
+    out_rows = g_ref.shape[1] // n_shard
+    heads_each = HEADS // n_rep
+    halves = heads_each // 2
+    slots = 2 * n_rep
+    rep = lax.axis_index("rep")
+    me = lax.axis_index("shard")
+    core = lax.rem(me, 2)
+    chip = me // 2
+    sib = me + 1 - 2 * core
+    other = 1 - core
+    slot = rep * 2 + core
+    sib_slot = rep * 2 + other
+
+    def remote(src, dst, send_sem, recv_sem, to_rep, to_shard):
+        return pltpu.make_async_remote_copy(
+            src_ref=src, dst_ref=dst, send_sem=send_sem, recv_sem=recv_sem,
+            device_id=(to_rep, to_shard), device_id_type=MESH,
+        )
+
+    def rep_at(step):
+        return lax.rem(rep + step, n_rep)
+
+    loads = [
+        pltpu.make_async_copy(src, dst, in_sem.at[i])
+        for i, (src, dst) in enumerate([
+            (k_hbm, kv.at[span, 0:rows, 0:half]),
+            (v_hbm, kv.at[span, 0:rows, half:2 * half]),
+            (seg_hbm, seg_ref),
+            (g_hbm, g_ref),
+            (q_hbm, q_ref),
+        ])
+    ]
+    for load in loads:
+        load.start()
+
+    barrier = pltpu.get_barrier_semaphore()
+    for step in range(1, n_shard):
+        pl.semaphore_signal(
+            barrier, inc=1, device_id=(rep, lax.rem(me + step, n_shard)), device_id_type=MESH
+        )
+    for step in range(1, n_rep):
+        for side in range(2):
+            pl.semaphore_signal(
+                barrier, inc=1, device_id=(rep_at(step), chip * 2 + side), device_id_type=MESH
+            )
+    for place in range(span):
+        @pl.when(me - span + place < 0)
+        def _(place=place):
+            kv[place] = jnp.zeros(kv.shape[1:], BF16)
+    kv[span, rows:rows + 16, :] = jnp.zeros((16, 2 * half), BF16)
+    for load in loads[:3]:
+        load.wait()
+    seg_row = seg_ref[...].astype(F32)
+    kv[span, rows:rows + 16, 0:rows] = jnp.broadcast_to(seg_row, (16, rows)).astype(BF16)
+    pl.semaphore_wait(barrier, (n_shard - 1) + 2 * (n_rep - 1))
+
+    def along(d):
+        return remote(
+            kv.at[span], kv.at[span - 2 * d], zk_send.at[d - 1], zk_recv.at[d - 1],
+            rep, me + 2 * d,
+        )
+
+    for d in range(1, reach + 1):
+        @pl.when(chip + d < n_chip)
+        def _(d=d):
+            along(d).start()
+
+    def across(d):
+        place = span + 1 - 2 * d
+        return remote(
+            kv.at[place + 1 - 2 * core], kv.at[place], sb_send.at[d - 1], sb_recv.at[d - 1],
+            rep, sib,
+        )
+
+    def across_exists(d):
+        return sib - 2 * d + 1 >= 0
+
+    @pl.when(core == 0)
+    def _():
+        across(1).start()
+
+    loads[3].wait()
+
+    gt_out[...] = g_ref[...].astype(F32).T.astype(BF16)
+
+    def lanes_of(index):
+        return gt.at[:, pl.ds(pl.multiple_of(index * rows, 128), rows)]
+
+    def g_copy(step):
+        to = sib if step == 0 else me
+        return remote(
+            gt_out, lanes_of(slot), g_send.at[step], g_recv.at[slot], rep_at(step), to
+        )
+
+    def g_hand(step):
+        index = rep_at(n_rep - step) * 2 + core
+        return remote(
+            lanes_of(index), lanes_of(index), f_send.at[step], g_recv.at[index], rep, sib
+        )
+
+    def g_arrived(index):
+        remote(gt_out, lanes_of(index), g_send.at[0], g_recv.at[index], rep, sib).wait_recv()
+
+    def g_rest():
+        g_arrived(sib_slot)
+        for step in range(1, n_rep):
+            g_arrived(rep_at(n_rep - step) * 2 + other)
+
+    for step in list(range(1, n_rep)) + [0]:
+        g_copy(step).start()
+    gt[:, pl.ds(pl.multiple_of(slot * rows, 128), rows)] = gt_out[...]
+
+    for d in range(1, reach + 1):
+        @pl.when(chip >= d)
+        def _(d=d):
+            along(d).wait_recv()
+        if d <= reach:
+            @pl.when((core == 1) & across_exists(d))
+            def _(d=d):
+                across(d).start()
+        if d + 1 <= reach:
+            @pl.when((core == 0) & across_exists(d + 1))
+            def _(d=d):
+                across(d + 1).start()
+    for d in range(1, reach + 1):
+        @pl.when(me - 2 * d + 1 >= 0)
+        def _(d=d):
+            across(d).wait_recv()
+
+    q_seg = jnp.broadcast_to(seg_row, (rows, rows)).T
+    for place in range(span + 1):
+        k_seg = kv[place, rows:rows + 16, 0:rows].astype(F32)[0:1]
+        allowed = q_seg == k_seg
+        if place == span:
+            q_at = lax.broadcasted_iota(jnp.int32, (rows, rows), 0)
+            k_at = lax.broadcasted_iota(jnp.int32, (rows, rows), 1)
+            allowed = allowed & (k_at <= q_at)
+        else:
+            block = lax.broadcasted_iota(jnp.int32, (rows, rows), 0) * 0 + (me - span + place)
+            allowed = allowed & (block >= 0)
+        bias[:, place * rows:(place + 1) * rows] = jnp.where(allowed, 0.0, -1e30)
+        for head in range(KVH):
+            lo = head * HD
+            span_rows = slice(place * rows, (place + 1) * rows)
+            kext[head, span_rows, :] = kv[place, 0:rows, lo:lo + HD]
+            vext[head, span_rows, 0:HD] = kv[place, 0:rows, KVH * HD + lo:KVH * HD + lo + HD]
+            vext[head, span_rows, HD:2 * HD] = jnp.ones((rows, HD), BF16)
+
+    loads[4].wait()
+
+    targets = [(step, side) for step in range(1, n_rep) for side in range(2)]
+    targets = targets + [(0, other), (0, core)]
+
+    def head_of(index, half):
+        step, side = targets[index]
+        return rep_at(step) * heads_each + side * halves + half
+
+    def a_copy(index, half):
+        step, side = targets[index]
+        lanes = pl.ds(pl.multiple_of(head_of(index, half) * HD, 128), HD)
+        return remote(
+            attn_vm.at[:, lanes], a_all.at[half, pl.ds(slot * rows, rows), :],
+            a_send.at[half * slots + index], a_recv.at[half * slots + slot],
+            rep_at(step), chip * 2 + side,
+        )
+
+    def a_arrived(source, half):
+        remote(
+            attn_vm.at[:, 0:HD], a_all.at[half, pl.ds(source * rows, rows), :],
+            a_send.at[0], a_recv.at[half * slots + source], rep, sib,
+        ).wait_recv()
+
+    def attend(index, half):
+        head = head_of(index, half)
+        group = head // (HEADS // KVH)
+        lanes = pl.ds(pl.multiple_of(head * HD, 128), HD)
+        s = lax.dot_general(
+            q_ref[:, lanes], kext[group], (((1,), (1,)), ((), ())),
+            preferred_element_type=F32,
+        ) + bias[...]
+        top = jnp.max(s, axis=-1, keepdims=True)
+        p = jnp.exp2((s - top) * SCALE).astype(BF16)
+        o = jnp.dot(p, vext[group], preferred_element_type=F32)
+        mixed = (o[:, 0:HD] / o[:, HD:2 * HD]).astype(BF16)
+        attn_vm[:, lanes] = mixed
+        if index == slots - 1:
+            a_all[half, pl.ds(slot * rows, rows), :] = mixed
+        else:
+            a_copy(index, half).start()
+
+    def p_copy(step, half):
+        to = lax.rem(me + step, n_shard)
+        return remote(
+            p_out.at[half, pl.ds(pl.multiple_of(to * out_rows, 16), out_rows), :],
+            z_in.at[half, me], p_send.at[half * n_shard + step],
+            p_recv.at[half * n_shard + me], rep, to,
+        )
+
+    def p_arrived(source, half):
+        remote(
+            p_out.at[half, 0:out_rows, :], z_in.at[half, source], p_send.at[0],
+            p_recv.at[half * n_shard + source], rep, sib,
+        ).wait_recv()
+
+    def term(half):
+        for step in range(1, n_rep):
+            for side in range(2):
+                a_arrived(rep_at(n_rep - step) * 2 + side, half)
+        a_arrived(sib_slot, half)
+        p_out[half] = jnp.dot(gt[...], a_all[half], preferred_element_type=F32).astype(BF16)
+        for step in range(1, n_shard):
+            p_copy(step, half).start()
+        z_in[half, me] = p_out[half, pl.ds(pl.multiple_of(me * out_rows, 16), out_rows), :]
+
+    def o_copy(step, half):
+        return remote(
+            o_all.at[half, rep], o_all.at[half, rep], o_send.at[half * n_rep + step],
+            o_recv.at[half * n_rep + rep], rep_at(step), me,
+        )
+
+    def share(half):
+        for step in range(1, n_shard):
+            p_arrived(lax.rem(me + step, n_shard), half)
+        for side in range(2):
+            total = z_in[half, side].astype(F32)
+            for source in range(1, n_chip):
+                total = total + z_in[half, 2 * source + side].astype(F32)
+            o_all[half, rep, :, side * HD:(side + 1) * HD] = total.astype(BF16)
+        for step in range(1, n_rep):
+            o_copy(step, half).start()
+
+    def finish(half):
+        for step in range(1, n_rep):
+            source = rep_at(step)
+            remote(
+                o_all.at[half, source], o_all.at[half, source], o_send.at[0],
+                o_recv.at[half * n_rep + source], rep, sib,
+            ).wait_recv()
+        for source in range(n_rep):
+            for side in range(2):
+                at = (source * heads_each + side * halves + half) * HD
+                gw_ref[:, at:at + HD] = o_all[
+                    half, source, :, side * HD:(side + 1) * HD
+                ].astype(F32)
+
+    for half in range(halves):
+        for index in range(slots):
+            attend(index, half)
+            if half == 0 and index >= slots - n_rep + 1:
+                step = index - (slots - n_rep)
+                g_arrived(rep_at(n_rep - step) * 2 + core)
+                g_hand(step).start()
+            if half > 0 and index == EARLY:
+                if half == 1:
+                    g_rest()
+                term(half - 1)
+    if halves == 1:
+        g_rest()
+    term(halves - 1)
+    out_copy = pltpu.make_async_copy(attn_vm, attn_hbm, out_sem)
+    out_copy.start()
+    for half in range(halves):
+        share(half)
+    for half in range(halves):
+        finish(half)
+
+    out_copy.wait()
+    for d in range(1, reach + 1):
+        @pl.when(chip + d < n_chip)
+        def _(d=d):
+            along(d).wait_send()
+
+        @pl.when(across_exists(d))
+        def _(d=d):
+            across(d).wait_send()
+    for step in range(n_rep):
+        g_copy(step).wait_send()
+        if step > 0:
+            g_hand(step).wait_send()
+    for half in range(halves):
+        for index in range(slots - 1):
+            a_copy(index, half).wait_send()
+        for step in range(1, n_shard):
+            p_copy(step, half).wait_send()
+        for step in range(1, n_rep):
+            o_copy(step, half).wait_send()
+
+
+def local_narrow(queries, keys, values, segments, grad_output):
     n_rep, n_shard = lax.axis_size("rep"), lax.axis_size("shard")
     rows = queries.shape[1]
     span = MOST // rows
@@ -278,14 +598,18 @@
     vmem = pl.BlockSpec(memory_space=pltpu.VMEM)
     dma = pltpu.SemaphoreType.DMA
     attn, grad_weight = pl.pallas_call(
-        functools.partial(kernel, n_rep, n_shard),
+        functools.partial(kernel_narrow, n_rep, n_shard),
         out_shape=(
             jax.ShapeDtypeStruct((rows, HEADS * HD), BF16),
             jax.ShapeDtypeStruct((out_rows, HEADS * HD), F32),
         ),
-        in_specs=[vmem] * 5,
+        in_specs=[pl.BlockSpec(memory_space=pltpu.HBM)] * 5,
         out_specs=(vmem, vmem),
         scratch_shapes=[
+            pltpu.VMEM((rows, HEADS * HD), BF16),
+            pltpu.VMEM((1, rows), jnp.int32),
+            pltpu.VMEM((rows, features), BF16),
+            dma((5,)),
             pltpu.VMEM((span + 1, rows + 16, 2 * KVH * HD), BF16),
             pltpu.VMEM((KVH, (span + 1) * rows, HD), BF16),
             pltpu.VMEM((KVH, (span + 1) * rows, 2 * HD), BF16),
@@ -301,10 +625,63 @@
             dma((n_chip,)), dma((n_chip,)), dma((n_rep,)), dma((n_rep,)),
         ],
         compiler_params=pltpu.CompilerParams(
-            collective_id=0, has_side_effects=True, vmem_limit_bytes=40 * 1024 * 1024
+            collective_id=0, has_side_effects=True, vmem_limit_bytes=63 * 1024 * 1024
         ),
     )(queries[0], keys[0], values[0], segments, grad_output[0])
     return attn[None], grad_weight
+
+
+def local_wide(queries, keys, values, segments, grad_output):
+    n_rep, n_shard = lax.axis_size("rep"), lax.axis_size("shard")
+    rows = queries.shape[1]
+    span = MOST // rows
+    reach = span // 2
+    features = grad_output.shape[2]
+    out_rows = features // n_shard
+    slots = 2 * n_rep
+    halves = HEADS // slots
+    vmem = pl.BlockSpec(memory_space=pltpu.VMEM)
+    dma = pltpu.SemaphoreType.DMA
+    attn, grad_weight = pl.pallas_call(
+        functools.partial(kernel, n_rep, n_shard),
+        out_shape=(
+            jax.ShapeDtypeStruct((rows, HEADS * HD), BF16),
+            jax.ShapeDtypeStruct((out_rows, HEADS * HD), F32),
+        ),
+        in_specs=[pl.BlockSpec(memory_space=pltpu.HBM)] * 5,
+        out_specs=(pl.BlockSpec(memory_space=pltpu.HBM), vmem),
+        scratch_shapes=[
+            pltpu.VMEM((rows, HEADS * HD), BF16),
+            pltpu.VMEM((1, rows), jnp.int32),
+            pltpu.VMEM((rows, features), BF16),
+            dma((5,)),
+            pltpu.VMEM((span + 1, rows + 16, 2 * KVH * HD), BF16),
+            pltpu.VMEM((KVH, (span + 1) * rows, HD), BF16),
+            pltpu.VMEM((KVH, (span + 1) * rows, 2 * HD), BF16),
+            pltpu.VMEM((rows, (span + 1) * rows), F32),
+            pltpu.VMEM((features, rows), BF16),
+            pltpu.VMEM((features, slots * rows), BF16),
+            pltpu.VMEM((rows, HEADS * HD), BF16),
+            pltpu.VMEM((halves, slots * rows, HD), BF16),
+            pltpu.VMEM((halves, features, HD), BF16),
+            pltpu.VMEM((halves, n_shard, out_rows, HD), BF16),
+            pltpu.VMEM((halves, n_rep, out_rows, 2 * HD), BF16),
+            dma((reach,)), dma((reach,)), dma((reach,)), dma((reach,)),
+            dma((n_rep,)), dma((slots,)), dma((halves * slots,)), dma((halves * slots,)),
+            dma((halves * n_shard,)), dma((halves * n_shard,)),
+            dma((halves * n_rep,)), dma((halves * n_rep,)), dma((n_rep,)), dma(()),
+        ],
+        compiler_params=pltpu.CompilerParams(
+            collective_id=1, has_side_effects=True, vmem_limit_bytes=63 * 1024 * 1024
+        ),
+    )(queries[0], keys[0], values[0], segments, grad_output[0])
+    return attn[None], grad_weight
+
+
+def local(*blocks):
+    if HEADS % (2 * lax.axis_size("rep")) == 0:
+        return local_wide(*blocks)
+    return local_narrow(*blocks)
 
 
 def solution(mesh):

time: 54.5 us -> 45.7 us (0.84)
  the two profiles are of different devices: /device:TPU:27 before, /device:TPU:0 now
where the time goes in v2:
time: 45.7 us; the launch traced here: 45.5 us
  Pallas kernels  41.9 us (92%)
  local copies, waits for them, and re-layouts  2.94 us (6%)
  between operations  0.65 us (1%)
    pallas_call x1, Pallas kernels, local_wide(): pl.pallas_call(functools.partial(kernel, n_rep, n_shard), out_shape=(jax....  41.9 us
    unnamed x4, local copies, waits for them, and re-layouts  2.94 us

profile of v2, /device:TPU:0, one launch (start us, length us, event | category | flops | bytes accessed | tf_op | source)
XLA Modules:
  0.0 45.5 jit_solution(11135053403314568472)
XLA Ops:
  0.6 41.9 %shard_map.68 = (bf16[128,2048]{1,0:T(8,128)(2,1)}, f32[128,2048]{1,0:T(8,128)}) custom-call(bf16[128,2048]{1,0:T(8,128)(2,1)} %bitcast.5, bf16[128,256]{1,0:T(8,128)(2,1)} %bitcast.8, bf16[128,256]{1,0:T(8,128)(2,1)} %bitcast.9, s32[1,128]{1,0:T(1,128)} %seg_hbm.1, bf16[128,1024]{1,0:T(8,128)(2,1)} %bitcast.7), custom_call_target="tpu_custom_call" | custom-call | tf_op jit(solution)/shard_map/pallas_call | solution.py:645
  42.6 0.0 copy-start
  42.6 2.0 %copy.9 = bf16[1,128,2048]{2,1,0:T(8,128)(2,1)} copy(bf16[1,128,2048]{2,1,0:T(8,128)(2,1)} %bitcast.6) | data formatting | bytes 1048576
  44.5 0.0 copy-done
  44.5 1.0 %copy.10 = f32[128,2048]{1,0:T(8,128)} copy(f32[128,2048]{1,0:T(8,128)S(1)} %copy-done) | data formatting | bytes 2097152
Async XLA Ops:
  42.6 2.0 %copy-start = (f32[128,2048]{1,0:T(8,128)S(1)}, f32[128,2048]{1,0:T(8,128)}, u32[]{:S(2)}) copy-start(f32[128,2048]{1,0:T(8,128)} %get-tuple-element.9) | copy-start | bytes 3145732

commit v3 on v2

--- a/solution.py
+++ b/solution.py
@@ -383,31 +383,55 @@
 
     gt_out[...] = g_ref[...].astype(F32).T.astype(BF16)
 
-    def lanes_of(index):
-        return gt.at[:, pl.ds(pl.multiple_of(index * rows, 128), rows)]
-
-    def g_copy(step):
-        to = sib if step == 0 else me
-        return remote(
-            gt_out, lanes_of(slot), g_send.at[step], g_recv.at[slot], rep_at(step), to
-        )
-
-    def g_hand(step):
-        index = rep_at(n_rep - step) * 2 + core
-        return remote(
-            lanes_of(index), lanes_of(index), f_send.at[step], g_recv.at[index], rep, sib
-        )
-
-    def g_arrived(index):
-        remote(gt_out, lanes_of(index), g_send.at[0], g_recv.at[index], rep, sib).wait_recv()
+    part = gt.shape[0] // 2
+
+    def lanes_of(index, piece):
+        return gt.at[
+            piece * part:(piece + 1) * part, pl.ds(pl.multiple_of(index * rows, 128), rows)
+        ]
+
+    def plane(axis):
+        bit = rep % 2 if axis != 1 else rep // 2
+        first = 1 - 2 * bit if axis == 0 else 2 - 4 * bit
+        if axis == 2:
+            first = 3 - 2 * rep
+        return rep + first
+
+    def g_copy(axis, piece):
+        to_rep, to = (rep, sib) if axis == 2 else (plane(axis), me)
+        return remote(
+            gt_out.at[piece * part:(piece + 1) * part], lanes_of(slot, piece),
+            g_send.at[2 * axis + piece], g_recv.at[2 * slot + piece], to_rep, to,
+        )
+
+    def g_corner(piece):
+        index = plane(piece) * 2 + core
+        return remote(
+            lanes_of(index, piece), lanes_of(index, piece), g_send.at[6 + piece],
+            g_recv.at[2 * index + piece], plane(1 - piece), me,
+        )
+
+    def g_hand(axis, piece):
+        index = plane(axis) * 2 + core
+        return remote(
+            lanes_of(index, piece), lanes_of(index, piece), f_send.at[2 * axis + piece],
+            g_recv.at[2 * index + piece], rep, sib,
+        )
+
+    def g_arrived(index, piece):
+        remote(
+            gt_out.at[0:part], lanes_of(index, piece), g_send.at[0],
+            g_recv.at[2 * index + piece], rep, sib,
+        ).wait_recv()
 
     def g_rest():
-        g_arrived(sib_slot)
-        for step in range(1, n_rep):
-            g_arrived(rep_at(n_rep - step) * 2 + other)
-
-    for step in list(range(1, n_rep)) + [0]:
-        g_copy(step).start()
+        for piece in range(2):
+            g_arrived(sib_slot, piece)
+            for axis in range(3):
+                g_arrived(plane(axis) * 2 + other, piece)
+
+    for axis, piece in [(0, 0), (1, 1), (0, 1), (1, 0), (2, 0), (2, 1)]:
+        g_copy(axis, piece).start()
     gt[:, pl.ds(pl.multiple_of(slot * rows, 128), rows)] = gt_out[...]
 
     for d in range(1, reach + 1):
@@ -426,6 +450,11 @@
         @pl.when(me - 2 * d + 1 >= 0)
         def _(d=d):
             across(d).wait_recv()
+
+    for piece in range(2):
+        g_arrived(plane(piece) * 2 + core, piece)
+        g_corner(piece).start()
+        g_hand(piece, piece).start()
 
     q_seg = jnp.broadcast_to(seg_row, (rows, rows)).T
     for place in range(span + 1):
@@ -546,10 +575,11 @@
     for half in range(halves):
         for index in range(slots):
             attend(index, half)
-            if half == 0 and index >= slots - n_rep + 1:
-                step = index - (slots - n_rep)
-                g_arrived(rep_at(n_rep - step) * 2 + core)
-                g_hand(step).start()
+            if half == 0 and index >= slots - 2:
+                hands = [(0, 1), (1, 0)] if index == slots - 2 else [(2, 0), (2, 1)]
+                for axis, piece in hands:
+                    g_arrived(plane(axis) * 2 + core, piece)
+                    g_hand(axis, piece).start()
             if half > 0 and index == EARLY:
                 if half == 1:
                     g_rest()
@@ -573,10 +603,11 @@
         @pl.when(across_exists(d))
         def _(d=d):
             across(d).wait_send()
-    for step in range(n_rep):
-        g_copy(step).wait_send()
-        if step > 0:
-            g_hand(step).wait_send()
+    for piece in range(2):
+        for axis in range(3):
+            g_copy(axis, piece).wait_send()
+            g_hand(axis, piece).wait_send()
+        g_corner(piece).wait_send()
     for half in range(halves):
         for index in range(slots - 1):
             a_copy(index, half).wait_send()
@@ -667,9 +698,9 @@
             pltpu.VMEM((halves, n_shard, out_rows, HD), BF16),
             pltpu.VMEM((halves, n_rep, out_rows, 2 * HD), BF16),
             dma((reach,)), dma((reach,)), dma((reach,)), dma((reach,)),
-            dma((n_rep,)), dma((slots,)), dma((halves * slots,)), dma((halves * slots,)),
+            dma((8,)), dma((2 * slots,)), dma((halves * slots,)), dma((halves * slots,)),
             dma((halves * n_shard,)), dma((halves * n_shard,)),
-            dma((halves * n_rep,)), dma((halves * n_rep,)), dma((n_rep,)), dma(()),
+            dma((halves * n_rep,)), dma((halves * n_rep,)), dma((6,)), dma(()),
         ],
         compiler_params=pltpu.CompilerParams(
             collective_id=1, has_side_effects=True, vmem_limit_bytes=63 * 1024 * 1024
@@ -679,7 +710,7 @@
 
 
 def local(*blocks):
-    if HEADS % (2 * lax.axis_size("rep")) == 0:
+    if lax.axis_size("rep") == 4:
         return local_wide(*blocks)
     return local_narrow(*blocks)
 

time: 45.7 us -> 46.9 us (1.026)
  Pallas kernels: 41.9 us -> 43.1 us
    pallas_call x1, Pallas kernels: 41.9 us -> 43.1 us  [local_wide(): pl.pallas_call(functools.partial(kernel, n_rep, n_shard), out_shape=(jax....]
where the time goes in v3:
time: 46.9 us; the launch traced here: 46.7 us
  Pallas kernels  43.1 us (92%)
  local copies, waits for them, and re-layouts  2.94 us (6%)
  between operations  0.65 us (1%)
    pallas_call x1, Pallas kernels, local_wide(): pl.pallas_call(functools.partial(kernel, n_rep, n_shard), out_shape=(jax....  43.1 us
    unnamed x4, local copies, waits for them, and re-layouts  2.94 us

profile of v3, /device:TPU:0, one launch (start us, length us, event | category | flops | bytes accessed | tf_op | source)
XLA Modules:
  0.0 46.7 jit_solution(467225957377721005)
XLA Ops:
  0.6 43.1 %shard_map.68 = (bf16[128,2048]{1,0:T(8,128)(2,1)}, f32[128,2048]{1,0:T(8,128)}) custom-call(bf16[128,2048]{1,0:T(8,128)(2,1)} %bitcast.5, bf16[128,256]{1,0:T(8,128)(2,1)} %bitcast.8, bf16[128,256]{1,0:T(8,128)(2,1)} %bitcast.9, s32[1,128]{1,0:T(1,128)} %seg_hbm.1, bf16[128,1024]{1,0:T(8,128)(2,1)} %bitcast.7), custom_call_target="tpu_custom_call" | custom-call | tf_op jit(solution)/shard_map/pallas_call | solution.py:676
  43.8 0.0 copy-start
  43.8 2.0 %copy.9 = bf16[1,128,2048]{2,1,0:T(8,128)(2,1)} copy(bf16[1,128,2048]{2,1,0:T(8,128)(2,1)} %bitcast.6) | data formatting | bytes 1048576
  45.7 0.0 copy-done
  45.7 1.0 %copy.10 = f32[128,2048]{1,0:T(8,128)} copy(f32[128,2048]{1,0:T(8,128)S(1)} %copy-done) | data formatting | bytes 2097152
Async XLA Ops:
  43.8 2.0 %copy-start = (f32[128,2048]{1,0:T(8,128)S(1)}, f32[128,2048]{1,0:T(8,128)}, u32[]{:S(2)}) copy-start(f32[128,2048]{1,0:T(8,128)} %get-tuple-element.9) | copy-start | bytes 3145732

commit v4 on v2

--- a/solution.py
+++ b/solution.py
@@ -406,29 +406,13 @@
         for step in range(1, n_rep):
             g_arrived(rep_at(n_rep - step) * 2 + other)
 
-    for step in list(range(1, n_rep)) + [0]:
+    for step in range(1, n_rep):
         g_copy(step).start()
     gt[:, pl.ds(pl.multiple_of(slot * rows, 128), rows)] = gt_out[...]
 
-    for d in range(1, reach + 1):
-        @pl.when(chip >= d)
-        def _(d=d):
-            along(d).wait_recv()
-        if d <= reach:
-            @pl.when((core == 1) & across_exists(d))
-            def _(d=d):
-                across(d).start()
-        if d + 1 <= reach:
-            @pl.when((core == 0) & across_exists(d + 1))
-            def _(d=d):
-                across(d + 1).start()
-    for d in range(1, reach + 1):
-        @pl.when(me - 2 * d + 1 >= 0)
-        def _(d=d):
-            across(d).wait_recv()
-
     q_seg = jnp.broadcast_to(seg_row, (rows, rows)).T
-    for place in range(span + 1):
+
+    def prepare(place):
         k_seg = kv[place, rows:rows + 16, 0:rows].astype(F32)[0:1]
         allowed = q_seg == k_seg
         if place == span:
@@ -446,6 +430,27 @@
             vext[head, span_rows, 0:HD] = kv[place, 0:rows, KVH * HD + lo:KVH * HD + lo + HD]
             vext[head, span_rows, HD:2 * HD] = jnp.ones((rows, HD), BF16)
 
+    prepare(span)
+
+    for d in range(1, reach + 1):
+        @pl.when(chip >= d)
+        def _(d=d):
+            along(d).wait_recv()
+        if d <= reach:
+            @pl.when((core == 1) & across_exists(d))
+            def _(d=d):
+                across(d).start()
+        if d + 1 <= reach:
+            @pl.when((core == 0) & across_exists(d + 1))
+            def _(d=d):
+                across(d + 1).start()
+    for d in range(1, reach + 1):
+        @pl.when(me - 2 * d + 1 >= 0)
+        def _(d=d):
+            across(d).wait_recv()
+    g_copy(0).start()
+    for place in range(span):
+        prepare(place)
     loads[4].wait()
 
     targets = [(step, side) for step in range(1, n_rep) for side in range(2)]
@@ -539,9 +544,7 @@
         for source in range(n_rep):
             for side in range(2):
                 at = (source * heads_each + side * halves + half) * HD
-                gw_ref[:, at:at + HD] = o_all[
-                    half, source, :, side * HD:(side + 1) * HD
-                ].astype(F32)
+                gw_ref[:, at:at + HD] = o_all[half, source, :, side * HD:(side + 1) * HD]
 
     for half in range(halves):
         for index in range(slots):
@@ -646,7 +649,7 @@
         functools.partial(kernel, n_rep, n_shard),
         out_shape=(
             jax.ShapeDtypeStruct((rows, HEADS * HD), BF16),
-            jax.ShapeDtypeStruct((out_rows, HEADS * HD), F32),
+            jax.ShapeDtypeStruct((out_rows, HEADS * HD), BF16),
         ),
         in_specs=[pl.BlockSpec(memory_space=pltpu.HBM)] * 5,
         out_specs=(pl.BlockSpec(memory_space=pltpu.HBM), vmem),
@@ -675,7 +678,7 @@
             collective_id=1, has_side_effects=True, vmem_limit_bytes=63 * 1024 * 1024
         ),
     )(queries[0], keys[0], values[0], segments, grad_output[0])
-    return attn[None], grad_weight
+    return attn[None], grad_weight.astype(F32)
 
 
 def local(*blocks):

time: 45.7 us -> 45.5 us (level)
  other arithmetic: 0 us -> 2.18 us
  local copies, waits for them, and re-layouts: 2.94 us -> 0.8 us
    convert_element_type x0 -> x1, other arithmetic: none -> 2.18 us  [local_wide(): return (attn[None], grad_weight.astype(F32))]
    unnamed x4 -> x3, local copies, waits for them, and re-layouts: 2.94 us -> 0.8 us
where the time goes in v4:
time: 45.5 us; the launch traced here: 45.4 us
  Pallas kernels  41.8 us (92%)
  other arithmetic  2.18 us (5%)
  local copies, waits for them, and re-layouts  0.8 us (2%)
  between operations  0.65 us (1%)
    pallas_call x1, Pallas kernels, local_wide(): pl.pallas_call(functools.partial(kernel, n_rep, n_shard), out_shape=(jax....  41.8 us
    convert_element_type x1, other arithmetic, local_wide(): return (attn[None], grad_weight.astype(F32))  2.18 us

profile of v4, /device:TPU:0, one launch (start us, length us, event | category | flops | bytes accessed | tf_op | source)
XLA Modules:
  0.0 45.4 jit_solution(11985014854451734561)
XLA Ops:
  0.6 41.8 %shard_map.68 = (bf16[128,2048]{1,0:T(8,128)(2,1)}, bf16[128,2048]{1,0:T(8,128)(2,1)}) custom-call(bf16[128,2048]{1,0:T(8,128)(2,1)} %bitcast.5, bf16[128,256]{1,0:T(8,128)(2,1)} %bitcast.8, bf16[128,256]{1,0:T(8,128)(2,1)} %bitcast.9, s32[1,128]{1,0:T(1,128)} %seg_hbm.1, bf16[128,1024]{1,0:T(8,128)(2,1)} %bitcast.7), custom_call_target="tpu_custom_call" | custom-call | tf_op jit(solution)/shard_map/pallas_call | solution.py:648
  42.4 0.0 copy-start
  42.4 2.2 %convert_element_type.3 = f32[128,2048]{1,0:T(8,128)} convert(bf16[128,2048]{1,0:T(8,128)(2,1)} %get-tuple-element.5) | non-fusion elementwise | flops 262144 | bytes 1572864 | tf_op jit(solution)/shard_map/convert_element_type | solution.py:681
  44.6 0.0 copy-done
  44.6 0.8 %copy.8 = bf16[1,128,2048]{2,1,0:T(8,128)(2,1)} copy(bf16[1,128,2048]{2,1,0:T(8,128)(2,1)S(1)} %bitcast.6) | data formatting | bytes 1048576
Async XLA Ops:
  42.4 2.2 %copy-start = (bf16[128,2048]{1,0:T(8,128)(2,1)S(1)}, bf16[128,2048]{1,0:T(8,128)(2,1)}, u32[]{:S(2)}) copy-start(bf16[128,2048]{1,0:T(8,128)(2,1)} %get-tuple-element.4) | copy-start | bytes 1572868
